TPU v7x, 128 devices: a whole 4x4x4 slice. The times are simulated.
128 devices in a mesh: dp: 32 (over y, x_hi, z), tensor: 4 (over x_lo, core).
Axes of the slice: x: 4 (x_hi: 2, x_lo: 2; x = x_hi * 2 + x_lo), y: 4, z: 4, core: 2. Of those that a mesh axis runs over, the one named last changes fastest.
Arguments:
- prompt_x: bfloat16 [4096, 5120], P('dp', 'tensor'), may hold values from -6 to 6
- prompt_bc: bfloat16 [4096, 512], P('dp'), may hold values from -6 to 6
- prompt_dt: float32 [80, 4096], P('tensor', 'dp'), may hold values from -2.5 to 6.5
- prompt_z: bfloat16 [4096, 5120], P('dp', 'tensor'), may hold values from -6 to 6
- resp_x: bfloat16 [16384, 5120], P('dp', 'tensor'), may hold values from -6 to 6
- resp_bc: bfloat16 [16384, 512], P('dp'), may hold values from -6 to 6
- resp_dt: float32 [80, 16384], P('tensor', 'dp'), may hold values from -2.5 to 6.5
- resp_z: bfloat16 [16384, 5120], P('dp', 'tensor'), may hold values from -6 to 6
- conv_x: float32 [4, 5120], P(None, 'tensor'), may hold values from -3 to 3
- conv_bc: float32 [4, 512], replicated, may hold values from -3 to 3
- head_params: float32 [3, 80], P(None, 'tensor'), may hold values from -8 to 1.5, as said below
- prompt_of: int32 [32], replicated, may hold values from 0 to 31, each once
- resp_len: int32 [32, 4], P('dp'), may hold values from 32 to 128, as said below
- prompt_cot: bfloat16 [4096, 5120], P('dp', 'tensor'), may hold values from -6 to 6
- resp_cot: bfloat16 [16384, 5120], P('dp', 'tensor'), may hold values from -6 to 6
Outputs:
- resp_out: bfloat16 [16384, 5120], P('dp', 'tensor')
- prompt_grad_x: bfloat16 [4096, 5120], P('dp', 'tensor')
- prompt_grad_bc: float32 [4096, 512], P('dp')
- prompt_grad_dt: float32 [80, 4096], P('tensor', 'dp')
- resp_grad_x: bfloat16 [16384, 5120], P('dp', 'tensor')
- resp_grad_bc: float32 [16384, 512], P('dp')
- resp_grad_dt: float32 [80, 16384], P('tensor', 'dp')
- conv_x_grad: float32 [4, 5120], P(None, 'tensor')
- conv_bc_grad: float32 [4, 512], replicated
- head_grads: float32 [3, 80], P(None, 'tensor')
Inputs may be any that keep to these rules, and one draw needn't show every extreme that they name: prompt_of is a permutation: every prompt is continued on exactly one dp index. `resp_len`: every dp index has at least one response of the full 128 tokens. `head_params`: row 0 is a log rate, row 1 a step bias below zero, row 2 a skip gain.
All inputs are finite; a program needn't handle non-finite values.
Results may differ from a plain program's by a relative error of at most 0.0045.
Values sent between devices are 32-bit elements; how exact they have to be, the bound alone decides.
A program may use at most 192 MiB of HBM per device.

v0:
```python
import functools
import types

import jax
import jax.numpy as jnp
from jax import lax
from jax.experimental import pallas as pl
from jax.experimental.pallas import tpu as pltpu
from jax.sharding import PartitionSpec as P

F32 = jnp.float32
BF = jnp.bfloat16
T = 128
NH = 20
NG = 10
NS = 256
CHD = 1280
BCW = 512
UNROLL = 5
ROW = 40
SMALL = 10


def mm(a, b, ca, cb):
    return lax.dot_general(a, b, (((ca,), (cb,)), ((), ())), preferred_element_type=F32)


def split2(a):
    hi = a.astype(BF)
    return hi, (a - hi.astype(F32)).astype(BF)


def split3(a):
    hi = a.astype(BF)
    rest = a - hi.astype(F32)
    mid = rest.astype(BF)
    return hi, mid, (rest - mid.astype(F32)).astype(BF)


def mm3(a, b, ca, cb):
    ah, al = split2(a)
    bh, bl = split2(b)
    return mm(ah, bh, ca, cb) + mm(ah, bl, ca, cb) + mm(al, bh, ca, cb)


def mmx(a, ones, ca, cb):
    hi, mid, lo = split3(a)
    return mm(hi, ones, ca, cb) + mm(mid, ones, ca, cb) + mm(lo, ones, ca, cb)


def sigmoid(v):
    return 0.5 + 0.5 * jnp.tanh(0.5 * v)


def softplus(u):
    e = jnp.exp(-jnp.abs(u))
    s = e / (2.0 + e)
    q = s * s
    poly = 1.0 + q * (1 / 3 + q * (1 / 5 + q * (1 / 7 + q * (1 / 9 + q * (1 / 11 + q / 13)))))
    return jnp.maximum(u, 0.0) + 2.0 * s * poly


def iota(shape, dim):
    return lax.broadcasted_iota(jnp.int32, shape, dim)


def fold8(a):
    return jnp.sum(a.reshape(16, 8, 128), axis=0)


BIG_IN = ("px", "pbc", "pdt", "cw", "cbc", "hp", "rdt", "pz", "pcot", "rz", "rcot", "rx", "rbc")
SCALARS = ("of", "rlen")
BIG_OUT = ("out", "pdx", "rdx", "rdbc", "o_pdbc", "o_pddt", "o_rddt", "o_cw", "o_cbc", "o_hp")
SHAPES = dict(
    px=((T, CHD), BF), pbc=((T, BCW), BF), pz=((T, CHD), BF), pcot=((T, CHD), BF),
    rx=((512, CHD), BF), rbc=((512, BCW), BF), rz=((512, CHD), BF), rcot=((512, CHD), BF),
    pdt=((NH, T), F32), rdt=((NH, 512), F32), cw=((4, CHD), F32), cbc=((4, BCW), F32), hp=((3, NH), F32),
    o_pdbc=((T, BCW), F32), o_pddt=((NH, T), F32), o_rddt=((NH, 512), F32), o_cw=((4, CHD), F32),
    o_cbc=((4, BCW), F32), o_hp=((3, NH), F32),
    out=((512, CHD), BF), pdx=((T, CHD), BF), rdx=((512, CHD), BF), rdbc=((512, BCW), F32),
)


def scratch_table():
    v = pltpu.VMEM
    dma = pltpu.SemaphoreType.DMA
    table = {name: v(*SHAPES[name]) for name in BIG_IN + BIG_OUT}
    for one in "tfbv":
        rows = {"t": SMALL, "f": ROW, "b": ROW, "v": SMALL}[one]
        for part in "shlr":
            table[one + part] = v((32, rows, 128), F32)
    table.update(
        hp_sum=v((4, 64, 128), F32), par_in=v((3, 4, 64, 128), F32), cb_in=v((4, 32, 128), F32), cb_out=v((32, 128), F32),
        rsum=v((512, BCW), F32), rrecv=v((4, 2, 64, BCW), F32),
        psum=v((T, BCW), F32), pfull=v((T, BCW), F32), precv=v((2, 64, BCW), F32),
        invv=v((1, 128), jnp.int32), inv=pltpu.SMEM((1, 128), jnp.int32),
        adt=v((NH, T), F32),
        dtr=v((6, NH, T), F32), sig=v((6, NH, T), F32), lr=v((6, NH, T), F32), cumr=v((6, NH, T), F32),
        tmp=v((6, 128, 128), F32), col=v((2, NH, 1), F32), dex=v((1, CHD), F32),
        cumB=v((6 * NH, T, T), F32), dtE=v((6 * T, CHD), F32),
        R=v((NG, 512, 128), BF), Gcol=v((12, T, T), F32), dGcol=v((12, T, T), F32),
        B=v((6, T, NS), F32), C=v((5, T, NS), F32), Cb=v((5, T, NS), BF), gpb=v((6 * T, BCW), F32),
        G=v((5, T, T), F32), dG=v((5, T, T), F32), acc=v((6, T, 128), F32), accq=v((T, 128), F32),
        xs=v((5, 136, 128), F32), ds=v((5, 144, 128), F32),
        tailx=v((8, CHD), F32), tailb=v((8, BCW), F32), dtailx=v((8, CHD), F32), dtailb=v((8, BCW), F32),
        dw=v((4, 8, CHD), F32), dwb=v((4, 8, BCW), F32), dD=v((8, CHD), F32),
        pxc=v((T, CHD), F32), pgp=v((T, CHD), F32), pdxf=v((T, CHD), F32),
        live=v((512, 128), F32), dy=v((512, CHD), F32), sz=v((512, CHD), F32),
        edy=v((512, CHD), BF), ee=v((512, CHD), F32),
        S=v((CHD, NS), BF), dS=v((CHD, NS), BF),
        dlr=v((NH, T), F32), ddr=v((NH, T), F32),
        sem=dma((8, 2, 32)), tsem=dma((16, 2)), gsem=dma((4, 2, 4)), isem=dma((len(BIG_IN) + 1,)), osem=dma((len(BIG_OUT),)),
    )
    return table


def kernel(n, nt, *refs):
    names = [name + "_in" for name in BIG_IN] + list(SCALARS)
    names += [name + "_out" for name in BIG_OUT] + list(scratch_table())
    K = types.SimpleNamespace(**dict(zip(names, refs)))
    me = lax.axis_index("dp")
    mt = lax.axis_index("tensor")
    left = iota((T, 128), 1) < 64
    lower = iota((T, T), 0) >= iota((T, T), 1)
    mesh_ids = pl.DeviceIdType.MESH
    many = n > 1

    if many:
        barrier = pltpu.get_barrier_semaphore()

        def greet(k):
            pl.semaphore_signal(barrier, inc=1, device_id={"dp": lax.rem(me + k, n)}, device_id_type=mesh_ids)

        pl.loop(1, n)(greet)
        for k in range(1, nt):
            pl.semaphore_signal(barrier, inc=1, device_id={"tensor": lax.rem(mt + k, nt)}, device_id_type=mesh_ids)

    loads = {
        name: pltpu.make_async_copy(getattr(K, name + "_in"), getattr(K, name), K.isem.at[i])
        for i, name in enumerate(BIG_IN)
    }
    for name in BIG_IN:
        loads[name].start()

    class Relay:
        def __init__(self, key, sem, table):
            self.s, self.h, self.l, self.r = (getattr(K, key + part) for part in "shlr")
            self.sem = sem
            self.table = table

        def copy(self, src, dst, sem):
            def one(k):
                peer = lax.rem(me + k, n)
                return pltpu.make_async_remote_copy(
                    src_ref=src.at[peer], dst_ref=dst.at[me], send_sem=K.sem.at[sem, 0, k], recv_sem=K.sem.at[sem, 1, k],
                    device_id={"dp": peer}, device_id_type=mesh_ids,
                )

            return one

        def send(self):
            if many:
                one = self.copy(self.s, self.h, self.sem)
                pl.loop(1, n)(lambda k: one(k).start())
                self.h[me] = self.s[me]

        def turn(self):
            if many:
                one = self.copy(self.s, self.h, self.sem)
                pl.loop(1, n)(lambda k: one(k).wait())

                def pick(d):
                    self.l[d] = self.h[self.table(d)]

                pl.loop(0, n)(pick)
                two = self.copy(self.l, self.r, self.sem + 1)
                pl.loop(1, n)(lambda k: two(k).start())
                self.r[me] = self.l[me]

        def end(self):
            if many:
                two = self.copy(self.l, self.r, self.sem + 1)
                pl.loop(1, n)(lambda k: two(k).wait())
            else:
                self.r[...] = self.s[...]

    forth = lambda d: K.of[d]
    home = lambda d: K.inv[0, d]
    rt, rf = Relay("t", 0, forth), Relay("f", 2, forth)
    rb, rd = Relay("b", 4, home), Relay("v", 6, home)

    def lanes_of(g):
        return pl.ds(pl.multiple_of(g * 128, 128), 128)

    def rows_of(q):
        return pl.ds(pl.multiple_of(q * T, T), T)

    def scatter_rows(ref, k, half, tile):
        spot = pl.ds(pl.multiple_of(8 * k, 8), 8)
        for i in range(16):
            ref[2 * i + half, spot, :] = tile[8 * i : 8 * i + 8, :]

    def gather_rows(ref, k, half):
        spot = pl.ds(pl.multiple_of(8 * k, 8), 8)
        return jnp.concatenate([ref[2 * i + half, spot, :] for i in range(16)], axis=0)

    def tail_rows(rows_x, rows_b):
        for r in range(42):
            i, m = divmod(r, 14)
            ref, m = (rows_x, m) if m < 10 else (rows_b, m - 10)
            yield r, ref, slice(5 + i, 6 + i), slice(128 * m, 128 * m + 128)

    for name in BIG_IN[:7]:
        loads[name].wait()
    K.tailx[...] = K.px[112:128, :].astype(F32)[8:16, :]
    K.tailb[...] = K.pbc[112:128, :].astype(F32)[8:16, :]
    K.ts[:, 8:10, :] = jnp.zeros((32, 2, 128), F32)
    for r, ref, row, lanes in tail_rows(K.tailx, K.tailb):
        K.ts[r // 2, 8 + r % 2 : 9 + r % 2, :] = ref[row, lanes]
    for h in range(NH):
        r = 42 + h
        K.ts[r // 2, 8 + r % 2 : 9 + r % 2, :] = K.pdt[h : h + 1, :]
    for half in range(2):
        scatter_rows(K.ts, 0, half, K.pbc[:, 128 * half : 128 * half + 128].astype(F32))

    def pack_x(k):
        for half in range(2):
            scatter_rows(K.fs, k, half, K.px[:, lanes_of(5 * half + k)].astype(F32))

    if many:
        pl.semaphore_wait(barrier, n - 1 + nt - 1)
    rt.send()
    pl.loop(0, 5)(pack_x)
    rf.send()

    tri = (iota((T, T), 0) <= iota((T, T), 1)).astype(F32).astype(BF)
    trir = (iota((T, T), 0) >= iota((T, T), 1)).astype(F32).astype(BF)
    tris = (iota((T, T), 0) < iota((T, T), 1)).astype(F32).astype(BF)
    eye = iota((NH, NH), 0) == iota((NH, NH), 1)

    lane = iota((1, 128), 1)
    back_to = jnp.zeros((1, 128), jnp.int32)
    for d in range(n):
        back_to = jnp.where(lane == K.of[d], d, back_to)
    K.invv[...] = back_to
    inv_copy = pltpu.make_async_copy(K.invv, K.inv, K.isem.at[len(BIG_IN)])
    inv_copy.start()

    def column(row):
        return jnp.sum(jnp.where(eye, jnp.broadcast_to(K.hp[row : row + 1, :], (NH, NH)), 0.0), axis=1, keepdims=True)

    K.col[0] = -jnp.exp(column(0))
    K.col[1] = column(1)
    for g in range(NG):
        K.dex[:, 128 * g : 128 * g + 128] = jnp.where(
            lane < 64, K.hp[2:3, 2 * g : 2 * g + 1], K.hp[2:3, 2 * g + 1 : 2 * g + 2]
        )
    for j in range(4):
        K.live[j * T : j * T + T, :] = jnp.where(iota((T, 128), 0) < K.rlen[0, j], 1.0, 0.0)

    def make_R(g):
        r = iota((512, 128), 0)
        want = 2 * g + jnp.where((r & 127) >= 64, 1, 0) + jnp.where(r >= 256, 32, 0)
        K.R[g] = (iota((512, 128), 1) == want).astype(F32).astype(BF)

    pl.loop(0, NG)(make_R)
    for name in ("dG", "acc", "accq", "dw", "dwb", "dD", "dtailx", "dtailb", "dGcol", "dlr", "ddr", "ds", "tmp"):
        ref = getattr(K, name)
        ref[...] = jnp.zeros(ref.shape, F32)

    def step_tables(dt_ref, ats, qs):
        every = list(zip(ats, qs))
        for at, q in every:
            u = dt_ref[:, at * T : at * T + T] + K.col[1]
            dt = softplus(u)
            lr = K.col[0] * dt
            cum = mmx(lr, tri, 1, 0)
            K.sig[q] = 1.0 / (1.0 + jnp.exp(-u))
            K.lr[q] = lr
            K.cumr[q] = cum
            K.tmp[q, 0:NH, :] = cum
            K.tmp[q, 32 : 32 + NH, :] = dt
        for at, q in every:
            cols = K.tmp[q].T
            for h in range(NH):
                K.cumB[q * NH + h] = jnp.broadcast_to(cols[:, h : h + 1], (T, T))
            for g in range(NG):
                a = 32 + 2 * g
                K.dtE[q * T : q * T + T, 128 * g : 128 * g + 128] = jnp.where(
                    left, jnp.broadcast_to(cols[:, a : a + 1], (T, 128)), jnp.broadcast_to(cols[:, a + 1 : a + 2], (T, 128))
                )

    def conv(x, tail, w, u=0):
        K.xs[u, 0:8, :] = tail
        K.xs[u, 8:136, :] = x
        v = w[0] * K.xs[u, 5:133, :] + w[1] * K.xs[u, 6:134, :] + w[2] * K.xs[u, 7:135, :] + w[3] * x
        s = sigmoid(v)
        xc = v * s
        return xc, s + xc * (1.0 - s)

    def conv_taps(dv, dw_ref, lanes, u=0):
        for k in range(4):
            dw_ref[k, :, lanes] += fold8(dv * K.xs[u, 5 + k : 133 + k, :])

    def tail_back(dv, w, tail_ref, lanes, u):
        K.ds[u, 8:16, :] = dv
        tail_ref[:, lanes] += w[0] * K.ds[u, 3:11, :] + w[1] * K.ds[u, 2:10, :] + w[2] * K.ds[u, 1:9, :]

    def conv_back(dv, w, u=0):
        K.ds[u, 8:136, :] = dv
        return w[3] * dv + w[2] * K.ds[u, 9:137, :] + w[1] * K.ds[u, 10:138, :] + w[0] * K.ds[u, 11:139, :]

    def taps(ref, lanes):
        return [ref[k : k + 1, lanes] for k in range(4)]

    no_tail = jnp.zeros((8, 128), F32)

    def bc_forward(bc_ref, at, q, tail, u=0):
        for m in range(4):
            lanes = slice(128 * m, 128 * m + 128)
            xc, gp = conv(bc_ref[rows_of(at), lanes].astype(F32), tail(lanes), taps(K.cbc, lanes), m)
            K.gpb[rows_of(q), lanes] = gp
            if m < 2:
                K.B[q, :, lanes] = xc
            else:
                half = slice(128 * (m - 2), 128 * (m - 2) + 128)
                K.C[q, :, half] = xc
                K.Cb[q, :, half] = xc.astype(BF)
        K.G[q] = jnp.where(lower, mm3(K.C[q], K.B[q], 1, 1), 0.0)

    def bc_back(bc_ref, at, q, tail, dc_more, o_ref):
        dgm = jnp.where(lower, K.dG[q], 0.0)
        dc = mm3(dgm, K.B[q], 1, 0) + dc_more
        db = mm3(dgm, K.C[q], 0, 0)
        for m in range(4):
            lanes = slice(128 * m, 128 * m + 128)
            d = db[:, lanes] if m < 2 else dc[:, 128 * (m - 2) : 128 * (m - 2) + 128]
            dv = d * K.gpb[rows_of(q), lanes]
            K.xs[m, 0:8, :] = tail(lanes)
            K.xs[m, 8:136, :] = bc_ref[rows_of(at), lanes].astype(F32)
            conv_taps(dv, K.dwb, lanes, m)
            o_ref[rows_of(at), lanes] = conv_back(dv, taps(K.cbc, lanes), m)

    def cum_pair(q, g):
        return jnp.where(left, K.cumB[q * NH + 2 * g], K.cumB[q * NH + 2 * g + 1])

    def attend(q, g, xc, dy, dt):
        xd = dt * xc
        x2 = jnp.concatenate([jnp.where(left, xd, 0.0).astype(BF), jnp.where(left, 0.0, xd).astype(BF)], axis=0)
        d2 = jnp.concatenate([jnp.where(left, dy, 0.0).astype(BF), jnp.where(left, 0.0, dy).astype(BF)], axis=0)
        xdb = xd.astype(BF)
        dyb = dy.astype(BF)
        scores = K.G[q]
        decay = [
            jnp.exp(jnp.minimum(K.cumB[q * NH + 2 * g + i] - K.cumr[q, pl.ds(2 * g + i, 1), :], 0.0)) for i in range(2)
        ]
        mix = [(scores * one).astype(BF) for one in decay]
        yin = mm(jnp.concatenate(mix, axis=1), x2, 1, 0)
        dxd = mm(jnp.concatenate(mix, axis=0), d2, 0, 0)
        dmix = mm(dyb, x2, 1, 1)
        K.dG[q] += dmix[:, :T] * decay[0] + dmix[:, T:] * decay[1]
        return yin, dxd, xdb.astype(F32), dyb.astype(F32)

    def reduce_heads(g, first, second=None):
        parts = list(split2(first))
        if second is not None:
            parts += split2(second)
        return mm(jnp.concatenate(parts, axis=1), K.R[g, : 128 * len(parts), :], 1, 0)

    def steps_back(q, o_ref, at):
        a = K.acc[q].T
        dlr = mmx(a[0:NH, :], trir, 1, 0)
        draw = (a[32 : 32 + NH, :] + K.col[0] * dlr) * K.sig[q]
        o_ref[:, pl.ds(pl.multiple_of(at * T, T), T)] = draw
        K.dlr[...] += K.lr[q] * dlr
        K.ddr[...] += draw

    def state_steps(acc, q):
        a = acc[...].T
        dlr = mmx(a[0:NH, :], tris, 1, 0)
        return dlr, (a[32 : 32 + NH, :] + K.col[0] * dlr) * K.sig[q]

    step_tables(K.pdt, [0], [0])
    bc_forward(K.pbc, 0, 0, lambda lanes: no_tail)
    loads["pz"].wait()
    loads["pcot"].wait()

    def prompt_local(i):
        for u in range(UNROLL):
            g = i * UNROLL + u
            lanes = lanes_of(g)
            w = taps(K.cw, lanes)
            xc, gp = conv(K.px[:, lanes].astype(F32), no_tail, w, u)
            K.pxc[:, lanes] = xc
            K.pgp[:, lanes] = gp
            z = K.pz[:, lanes].astype(F32)
            dy = K.pcot[:, lanes].astype(F32) * (z * sigmoid(z))
            dt = K.dtE[0:T, lanes]
            yin, dxd, xdr, dyr = attend(0, g, xc, dy, dt)
            K.acc[0] += reduce_heads(g, dyr * yin - xdr * dxd, xc * dxd)
            K.dD[:, lanes] += fold8(dy * xc)
            dv = (dt * dxd + K.dex[:, lanes] * dy) * gp
            conv_taps(dv, K.dw, lanes, u)
            K.pdxf[:, lanes] = conv_back(dv, w, u)

    pl.loop(0, NG // UNROLL)(prompt_local)
    bc_back(K.pbc, 0, 0, lambda lanes: no_tail, 0.0, K.psum)
    steps_back(0, K.o_pddt, 0)

    rt.turn()

    step_tables(K.rdt, [0, 1, 2, 3], [1, 2, 3, 4])
    loads["rz"].wait()
    loads["rcot"].wait()

    def gates(i):
        j = i // NG
        g = lax.rem(i, NG)
        lanes = lanes_of(g)
        rows = rows_of(j)
        z = K.rz[rows, lanes].astype(F32)
        sz = z * sigmoid(z)
        dy = K.rcot[rows, lanes].astype(F32) * (sz * K.live[rows, :])
        e = jnp.exp(cum_pair(j + 1, g))
        K.sz[rows, lanes] = sz
        K.dy[rows, lanes] = dy
        K.ee[rows, lanes] = e
        K.edy[rows, lanes] = (e * dy).astype(BF)

    pl.loop(0, 4 * NG, unroll=2)(gates)
    rf.turn()
    loads["rx"].wait()
    loads["rbc"].wait()
    inv_copy.wait()
    rt.end()

    for r, ref, row, lanes in tail_rows(K.tailx, K.tailb):
        ref[row, lanes] = K.tr[r // 2, 8 + r % 2 : 9 + r % 2, :]
    for h in range(NH):
        r = 42 + h
        K.adt[h : h + 1, :] = K.tr[r // 2, 8 + r % 2 : 9 + r % 2, :]
    for j in range(4):
        bc_forward(K.rbc, j, j + 1, lambda lanes: K.tailb[:, lanes])
    for half in range(2):
        lanes = slice(128 * half, 128 * half + 128)
        xc, gp = conv(gather_rows(K.tr, 0, half), no_tail, taps(K.cbc, lanes), half)
        K.B[5, :, lanes] = xc
        K.gpb[5 * T : 6 * T, lanes] = gp

    def state_grad(k):
        bh = K.B[5].astype(BF)
        for half in range(2):
            lanes = lanes_of(5 * half + k)
            ds = mm(K.edy[:, lanes], K.Cb[1:5].reshape(4 * T, NS), 0, 0).astype(BF)
            K.dS[lanes, :] = ds
            scatter_rows(K.bs, k, half, mm(bh, ds, 1, 1))

    pl.loop(0, 5)(state_grad)
    rb.send()
    step_tables(K.adt, [0], [5])

    row8 = iota((8, 128), 0)
    for j in range(4):
        for t in range(3):
            K.Gcol[3 * j + t] = jnp.broadcast_to(K.G[j + 1, :, t : t + 1], (T, T))

    def first_rows(j):
        def five(i):
            for u in range(UNROLL):
                g = i * UNROLL + u
                lanes = lanes_of(g)
                w = taps(K.cw, lanes)
                K.xs[u, 0:8, :] = K.tailx[:, lanes]
                K.xs[u, 8:24, :] = K.rx[pl.ds(j * T, 16), lanes].astype(F32)
                v = (w[0] * K.xs[u, 5:13, :] + w[1] * K.xs[u, 6:14, :] + w[2] * K.xs[u, 7:15, :]
                     + w[3] * K.xs[u, 8:16, :])
                sg = sigmoid(v)
                xc = v * sg
                gp = sg + xc * (1.0 - sg)
                dt = K.dtE[pl.ds((j + 1) * T, 8), lanes]
                xd = dt * xc
                dy = K.dy[rows_of(j), lanes]
                cum = cum_pair(j + 1, g)
                dxd = jnp.zeros((8, 128), F32)
                for t in range(3):
                    m = jnp.exp(jnp.minimum(cum - cum[t : t + 1, :], 0.0)) * dy
                    K.dGcol[3 * j + t] += m * xd[t : t + 1, :]
                    dxd = jnp.where(row8 == t, jnp.sum(K.Gcol[3 * j + t] * m, axis=0, keepdims=True), dxd)
                dv = (dt * dxd + K.dex[:, lanes] * dy[0:8, :]) * gp
                tail_back(jnp.where(row8 < 3, dv, 0.0), w, K.dtailx, lanes, u)

        pl.loop(0, NG // UNROLL)(five)

    def first_bc_rows(j):
        more = mm(K.edy[pl.ds(j * T, 16), :], K.S[...], 1, 0)[0:8, :]
        r8 = iota((8, NS), 0)
        dc = more
        db = jnp.zeros((8, NS), F32)
        for t in range(3):
            col = jnp.sum(K.dGcol[3 * j + t], axis=1, keepdims=True)
            col = jnp.where(iota((T, 1), 0) >= t, col, 0.0)
            dc = dc + col[0:8, :] * K.B[j + 1, t : t + 1, :]
            db = jnp.where(r8 == t, jnp.sum(col * K.C[j + 1], axis=0, keepdims=True), db)
        for m in range(4):
            lanes = slice(128 * m, 128 * m + 128)
            d = db[:, lanes] if m < 2 else dc[:, 128 * (m - 2) : 128 * (m - 2) + 128]
            dv = jnp.where(row8 < 3, d * K.gpb[pl.ds((j + 1) * T, 8), lanes], 0.0)
            tail_back(dv, taps(K.cbc, lanes), K.dtailb, lanes, m)

    for j in range(4):
        first_rows(j)

    def resp_local(j):
        def five(i):
            for u in range(UNROLL):
                g = i * UNROLL + u
                lanes = lanes_of(g)
                rows = rows_of(j)
                w = taps(K.cw, lanes)
                xc, gp = conv(K.rx[rows, lanes].astype(F32), K.tailx[:, lanes], w, u)
                dy = K.dy[rows, lanes]
                dt = K.dtE[rows_of(j + 1), lanes]
                yin, dxd, xdr, dyr = attend(j + 1, g, xc, dy, dt)
                gain = K.dex[:, lanes]
                y = yin + gain * xc
                steps = dyr * yin - xdr * dxd
                cs = mm(K.Cb[j + 1], K.S[lanes, :], 1, 1)
                K.out[rows, lanes] = ((y + K.ee[rows, lanes] * cs) * K.sz[rows, lanes]).astype(BF)
                steps = steps + K.edy[rows, lanes].astype(F32) * cs
                K.acc[j + 1] += reduce_heads(g, steps, xc * dxd)
                K.dD[:, lanes] += fold8(dy * xc)
                dv = (dt * dxd + gain * dy) * gp
                conv_taps(dv, K.dw, lanes, u)
                K.rdx[rows, lanes] = conv_back(dv, w, u).astype(BF)

        pl.loop(0, NG // UNROLL)(five)

    def resp_bc_back(j):
        more = mm(K.edy[rows_of(j), :], K.S[...], 1, 0)
        bc_back(K.rbc, j, j + 1, lambda lanes: K.tailb[:, lanes], more, K.rsum)

    core = lax.rem(mt, 2)
    mate = mt + 1 - 2 * core
    across = lax.rem(mt + 2, 4)

    class TensorSum:
        def __init__(self, buf, full, recv, base, at):
            mine = pl.ds(pl.multiple_of(base + core * 64, 8), 64)
            other = pl.ds(pl.multiple_of(base + (1 - core) * 64, 8), 64)
            self.buf, self.full, self.recv, self.base, self.mine = buf, full, recv, base, mine
            plan = ((buf.at[other, :], recv.at[0], mate), (buf.at[mine, :], recv.at[1], across),
                    (buf.at[mine, :], full.at[mine, :], mate))
            self.steps = [
                pltpu.make_async_remote_copy(
                    src_ref=src, dst_ref=dst, send_sem=K.tsem.at[at + i, 0], recv_sem=K.tsem.at[at + i, 1],
                    device_id={"tensor": peer}, device_id_type=mesh_ids,
                )
                for i, (src, dst, peer) in enumerate(plan)
            ] if many else None

        def go(self, stage):
            if not many:
                if stage == 0:
                    rows = pl.ds(self.base, T)
                    self.full[rows, :] = self.buf[rows, :]
                return
            if stage > 0:
                self.steps[stage - 1].wait()
            if stage in (1, 2):
                self.buf[self.mine, :] += self.recv[stage - 1]
            if stage == 2:
                self.full[self.mine, :] = self.buf[self.mine, :]
            if stage < 3:
                self.steps[stage].start()

    sums = [TensorSum(K.rsum, K.rdbc, K.rrecv.at[j], j * T, 3 * j) for j in range(4)]

    rf.end()

    def adopt(k, dbp):
        bh, bl = split2(K.B[5])
        for half in range(2):
            g = 5 * half + k
            lanes = lanes_of(g)
            xc, gp = conv(gather_rows(K.fr, k, half), no_tail, taps(K.cw, lanes), half)
            cum = cum_pair(5, g)
            lv = jnp.exp(cum[T - 1 : T, :] - cum)
            dt = K.dtE[5 * T : 6 * T, lanes]
            xd = dt * xc
            xh, xl = split2(lv * xd)
            K.S[lanes, :] = (mm(xh, bh, 0, 0) + mm(xh, bl, 0, 0) + mm(xl, bh, 0, 0)).astype(BF)
            dbp = dbp + mm(xh, K.dS[lanes, :], 1, 0)
            lu = lv * gather_rows(K.bs, k, half)
            K.acc[5] += reduce_heads(g, xd * lu, xc * lu)
            conv_taps(dt * lu * gp, K.dw, lanes, half)
        return dbp

    dbp = lax.fori_loop(0, 5, adopt, jnp.zeros((T, NS), F32))
    for half in range(2):
        lanes = slice(128 * half, 128 * half + 128)
        scatter_rows(K.vs, 0, half, dbp[:, lanes])
        K.xs[half, 0:8, :] = no_tail
        K.xs[half, 8:136, :] = gather_rows(K.tr, 0, half)
        conv_taps(dbp[:, lanes] * K.gpb[5 * T : 6 * T, lanes], K.dwb, lanes, half)
    for j in range(4):
        first_bc_rows(j)
    K.vs[:, 8:10, :] = jnp.zeros((32, 2, 128), F32)
    for r, ref, row, lanes in tail_rows(K.dtailx, K.dtailb):
        K.vs[r // 2, 8 + r % 2 : 9 + r % 2, :] = ref[row, lanes]
    rd.send()
    dlr, draw = state_steps(K.acc.at[5], 5)
    K.dlr[...] += K.lr[5] * dlr
    K.ddr[...] += draw

    resp_local(0)
    resp_bc_back(0)
    sums[0].go(0)
    rb.turn()
    resp_local(1)
    resp_bc_back(1)
    sums[0].go(1)
    sums[1].go(0)
    rd.turn()
    resp_local(2)
    resp_bc_back(2)
    sums[0].go(2)
    sums[1].go(1)
    sums[2].go(0)
    resp_local(3)
    resp_bc_back(3)
    sums[3].go(0)
    sums[1].go(2)
    sums[2].go(1)
    store_rdx = pltpu.make_async_copy(K.rdx, K.rdx_out, K.osem.at[0])
    store_rdx.start()
    store_out = pltpu.make_async_copy(K.out, K.out_out, K.osem.at[1])
    store_out.start()

    for j in range(4):
        steps_back(j + 1, K.o_rddt, j)
    K.hp_sum[0] = jnp.zeros((64, 128), F32)
    for k in range(4):
        total = jnp.sum(K.dw[k], axis=0, keepdims=True)
        for g in range(NG):
            K.hp_sum[0, k * NG + g : k * NG + g + 1, :] = total[:, 128 * g : 128 * g + 128]
        total = jnp.sum(K.dwb[k], axis=0, keepdims=True)
        for m in range(4):
            K.hp_sum[0, 40 + 4 * k + m : 41 + 4 * k + m, :] = total[:, 128 * m : 128 * m + 128]
    skip = jnp.zeros((8, 128), F32)
    for g in range(NG):
        skip = skip + mm(jnp.concatenate(split2(K.dD[:, 128 * g : 128 * g + 128]), axis=1), K.R[g, :256, :], 1, 0)
    spread_eye = iota((NH, 128), 0) == iota((NH, 128), 1)

    def as_row(ref):
        total = jnp.sum(ref[...], axis=1, keepdims=True)
        return jnp.sum(jnp.where(spread_eye, jnp.broadcast_to(total, (NH, 128)), 0.0), axis=0, keepdims=True)

    K.hp_sum[0, 56:57, :] = as_row(K.dlr)
    K.hp_sum[0, 57:58, :] = as_row(K.ddr)
    K.hp_sum[0, 58:59, :] = jnp.sum(skip, axis=0, keepdims=True)

    z_at, x_at, y_at = lax.rem(me, 4), lax.rem(me // 4, 2), me // 8
    axes = (
        (4, z_at, lambda k: {"dp": me - z_at + lax.rem(z_at + k, 4)}),
        (4, y_at, lambda k: {"dp": me - 8 * y_at + 8 * lax.rem(y_at + k, 4)}),
        (2, x_at, lambda k: {"dp": me + 4 - 8 * x_at}),
    )

    def exchange(src, hold, size, at, peer, sem):
        return [
            pltpu.make_async_remote_copy(
                src_ref=src, dst_ref=hold.at[at], send_sem=K.gsem.at[sem, 0, k], recv_sem=K.gsem.at[sem, 1, k],
                device_id=peer(k), device_id_type=mesh_ids,
            )
            for k in range(1, size)
        ]

    def param_step(i, start):
        size, at, peer = axes[i]
        if not many:
            if not start:
                K.hp_sum[i + 1] = K.hp_sum[i]
            return
        copies = exchange(K.hp_sum.at[i], K.par_in.at[i], size, at, peer, i)
        if start:
            for one in copies:
                one.start()
            K.par_in[i, at] = K.hp_sum[i]
        else:
            for one in copies:
                one.wait()
            total = K.par_in[i, 0]
            for k in range(1, size):
                total = total + K.par_in[i, k]
            K.hp_sum[i + 1] = total

    param_step(0, True)
    rd.end()
    for half in range(2):
        lanes = slice(128 * half, 128 * half + 128)
        dv = gather_rows(K.vr, 0, half) * K.gpb[0:T, lanes]
        K.psum[:, lanes] += conv_back(dv, taps(K.cbc, lanes), u=half)
    prompt_sum = TensorSum(K.psum, K.pfull, K.precv, 0, 12)
    prompt_sum.go(0)
    sums[3].go(1)
    sums[2].go(2)
    param_step(0, False)
    param_step(1, True)

    def prompt_final(k):
        for half in range(2):
            g = 5 * half + k
            lanes = lanes_of(g)
            cum = cum_pair(0, g)
            lu = jnp.exp(cum[T - 1 : T, :] - cum) * gather_rows(K.br, k, half)
            dt = K.dtE[0:T, lanes]
            xlu = K.pxc[:, lanes] * lu
            K.accq[...] += reduce_heads(g, dt * xlu, xlu)
            K.pdxf[:, lanes] += conv_back(dt * lu * K.pgp[:, lanes], taps(K.cw, lanes), u=half)

    rb.end()
    pl.loop(0, 5)(prompt_final)
    K.tailx[...] = jnp.zeros((8, CHD), F32)
    K.tailb[...] = jnp.zeros((8, BCW), F32)
    for r, ref, row, lanes in tail_rows(K.tailx, K.tailb):
        ref[row, lanes] = K.vr[r // 2, 8 + r % 2 : 9 + r % 2, :]
    K.pdxf[120:128, :] += K.tailx[...]
    K.pdx[...] = K.pdxf[...].astype(BF)
    store_pdx = pltpu.make_async_copy(K.pdx, K.pdx_out, K.osem.at[3])
    store_pdx.start()
    prompt_sum.go(1)
    param_step(1, False)
    param_step(2, True)
    sums[3].go(2)
    K.o_pddt[...] += state_steps(K.accq, 0)[1]
    param_step(2, False)
    prompt_sum.go(2)
    for j in range(4):
        sums[j].go(3)
    store_rdbc = pltpu.make_async_copy(K.rdbc, K.rdbc_out, K.osem.at[2])
    store_rdbc.start()

    K.cb_out[0:16, :] = jnp.zeros((16, 128), F32)
    for i in range(3):
        for m in range(4):
            K.cb_out[4 * i + m : 4 * i + m + 1, :] = K.tailb[5 + i : 6 + i, 128 * m : 128 * m + 128]
    K.cb_out[16:32, :] = K.hp_sum[3, 40:56, :]
    if many:
        last = exchange(K.cb_out, K.cb_in, nt, mt, lambda k: {"tensor": lax.rem(mt + k, nt)}, 3)
        for one in last:
            one.start()
        K.cb_in[mt] = K.cb_out[...]
    for k in range(4):
        for g in range(NG):
            K.o_cw[k : k + 1, 128 * g : 128 * g + 128] = K.hp_sum[3, k * NG + g : k * NG + g + 1, :]
    K.o_hp[...] = K.hp_sum[3, 56:59, 0:NH]
    prompt_sum.go(3)
    K.o_pdbc[...] = K.pfull[...]
    if many:
        for one in last:
            one.wait()
        total = K.cb_in[0]
        for k in range(1, nt):
            total = total + K.cb_in[k]
    else:
        total = K.cb_out[...]
    for m in range(4):
        lanes = slice(128 * m, 128 * m + 128)
        for i in range(3):
            K.o_pdbc[125 + i : 126 + i, lanes] += total[4 * i + m : 4 * i + m + 1, :]
        for k in range(4):
            K.o_cbc[k : k + 1, lanes] = total[16 + 4 * k + m : 17 + 4 * k + m, :]
    stores = [store_rdx, store_out, store_rdbc, store_pdx]
    for i, name in enumerate(BIG_OUT[4:]):
        one = pltpu.make_async_copy(getattr(K, name), getattr(K, name + "_out"), K.osem.at[4 + i])
        one.start()
        stores.append(one)
    for one in stores:
        one.wait()


def finish(*refs):
    count = len(refs) // 3
    sems = refs[-1]
    come = [pltpu.make_async_copy(refs[i], refs[2 * count + i], sems.at[0, i]) for i in range(count)]
    leave = [pltpu.make_async_copy(refs[2 * count + i], refs[count + i], sems.at[1, i]) for i in range(count)]
    for one in come:
        one.start()
    for one, two in zip(come, leave):
        one.wait()
        two.start()
    for one in leave:
        one.wait()


def body(n, nt, *args):
    (px, pbc, pdt, pz, rx, rbc, rdt, rz, cw, cbc, hp, of, rlen, pcot, rcot) = args
    given = dict(px=px, pbc=pbc, pdt=pdt, pz=pz, pcot=pcot, rx=rx, rbc=rbc, rdt=rdt, rz=rz, rcot=rcot, cw=cw, cbc=cbc, hp=hp)
    sm = pl.BlockSpec(memory_space=pltpu.SMEM)
    far = pl.BlockSpec(memory_space=pl.ANY)
    shape = jax.ShapeDtypeStruct
    params = dict(vmem_limit_bytes=62 * 1024 * 1024, has_side_effects=True)
    if n > 1:
        params["collective_id"] = 0
    shapes = [shape(*SHAPES[name]) for name in BIG_OUT]
    results = pl.pallas_call(
        functools.partial(kernel, n, nt),
        out_shape=tuple(shapes),
        in_specs=[far] * len(BIG_IN) + [sm] * len(SCALARS),
        out_specs=tuple([far] * len(BIG_OUT)),
        scratch_shapes=list(scratch_table().values()),
        compiler_params=pltpu.CompilerParams(**params),
    )(*[given[name] for name in BIG_IN], of, rlen)
    results = pl.pallas_call(
        finish,
        out_shape=tuple(shapes),
        in_specs=[far] * len(shapes),
        out_specs=tuple([far] * len(shapes)),
        scratch_shapes=[pltpu.VMEM(one.shape, one.dtype) for one in shapes] + [pltpu.SemaphoreType.DMA((2, len(shapes)))],
        compiler_params=pltpu.CompilerParams(vmem_limit_bytes=62 * 1024 * 1024),
    )(*results)
    got = dict(zip(BIG_OUT, results))
    order = ("out", "pdx", "o_pdbc", "o_pddt", "rdx", "rdbc", "o_rddt", "o_cw", "o_cbc", "o_hp")
    return tuple(got[name] for name in order)


def solution(mesh):
    n = mesh.shape["dp"]
    nt = mesh.shape["tensor"]
    placed = (
        P("dp", "tensor"), P("dp", None), P("tensor", "dp"), P("dp", "tensor"),
        P("dp", "tensor"), P("dp", None), P("tensor", "dp"), P("dp", "tensor"),
        P(None, "tensor"), P(), P(None, "tensor"), P(), P("dp", None),
        P("dp", "tensor"), P("dp", "tensor"),
    )
    return jax.shard_map(
        functools.partial(body, n, nt),
        mesh=mesh,
        in_specs=placed,
        out_specs=(
            P("dp", "tensor"), P("dp", "tensor"), P("dp", None), P("tensor", "dp"),
            P("dp", "tensor"), P("dp", None), P("tensor", "dp"),
            P(None, "tensor"), P(), P(None, "tensor"),
        ),
        check_vma=False,
    )
```

profile of v0, /device:TPU:0, one launch (start us, length us, event | category | flops | bytes accessed | tf_op | source)
XLA Modules:
  0.0 85.9 jit_solution(18008399457939163326)
XLA Ops:
  0.6 81.6 %shard_map.222 = (bf16[512,1280]{1,0:T(8,128)(2,1)}, bf16[128,1280]{1,0:T(8,128)(2,1)}, bf16[512,1280]{1,0:T(8,128)(2,1)}, f32[512,512]{1,0:T(8,128)}, f32[128,5...) custom-call(bf16[128,1280]{1,0:T(8,128)(2,1)} %refs_0_.1, ...), custom_call_target="tpu_custom_call" | custom-call | tf_op jit(solution)/shard_map/pallas_call | solution.py:806
  82.3 3.5 %shard_map.223 = (bf16[512,1280]{1,0:T(8,128)(2,1)}, bf16[128,1280]{1,0:T(8,128)(2,1)}, bf16[512,1280]{1,0:T(8,128)(2,1)}, f32[512,512]{1,0:T(8,128)}, f32[128,5...) custom-call(bf16[512,1280]{1,0:T(8,128)(2,1)} %get-tuple-element.30., ...), custom_call_target="tpu_custom_call" | custom-call | tf_op jit(solution)/shard_map/pallas_call | solution.py:814
where the time goes:
time: 87.1 us; the launch traced here: 85.9 us
  Pallas kernels  85.1 us (98%)
    pallas_call x1, Pallas kernels, body(): pl.pallas_call(functools.partial(kernel, n, nt), out_shape=tuple(shapes),...  81.6 us
    pallas_call x1, Pallas kernels, body(): pl.pallas_call(finish, out_shape=tuple(shapes), in_specs=[far] * len(shap...  3.53 us

commit v1 on v0

--- a/solution.py
+++ b/solution.py
@@ -16,7 +16,7 @@
 NS = 256
 CHD = 1280
 BCW = 512
-UNROLL = 5
+UNROLL = 10
 ROW = 40
 SMALL = 10
 
@@ -101,7 +101,7 @@
         R=v((NG, 512, 128), BF), Gcol=v((12, T, T), F32), dGcol=v((12, T, T), F32),
         B=v((6, T, NS), F32), C=v((5, T, NS), F32), Cb=v((5, T, NS), BF), gpb=v((6 * T, BCW), F32),
         G=v((5, T, T), F32), dG=v((5, T, T), F32), acc=v((6, T, 128), F32), accq=v((T, 128), F32),
-        xs=v((5, 136, 128), F32), ds=v((5, 144, 128), F32),
+        xs=v((10, 136, 128), F32), ds=v((10, 144, 128), F32),
         tailx=v((8, CHD), F32), tailb=v((8, BCW), F32), dtailx=v((8, CHD), F32), dtailb=v((8, BCW), F32),
         dw=v((4, 8, CHD), F32), dwb=v((4, 8, BCW), F32), dD=v((8, CHD), F32),
         pxc=v((T, CHD), F32), pgp=v((T, CHD), F32), pdxf=v((T, CHD), F32),

time: 87.1 us -> 85.8 us (0.985)
  Pallas kernels: 85.1 us -> 83.8 us
    pallas_call x1, Pallas kernels: 81.6 us -> 80.3 us  [body(): pl.pallas_call(functools.partial(kernel, n, nt), out_shape=tuple(shapes),...]
where the time goes in v1:
time: 85.8 us; the launch traced here: 84.6 us
  Pallas kernels  83.8 us (98%)
    pallas_call x1, Pallas kernels, body(): pl.pallas_call(functools.partial(kernel, n, nt), out_shape=tuple(shapes),...  80.3 us
    pallas_call x1, Pallas kernels, body(): pl.pallas_call(finish, out_shape=tuple(shapes), in_specs=[far] * len(shap...  3.53 us

profile of v1, /device:TPU:0, one launch (start us, length us, event | category | flops | bytes accessed | tf_op | source)
XLA Modules:
  0.0 84.6 jit_solution(2050575567434931433)
XLA Ops:
  0.6 80.3 %shard_map.222 = (bf16[512,1280]{1,0:T(8,128)(2,1)}, bf16[128,1280]{1,0:T(8,128)(2,1)}, bf16[512,1280]{1,0:T(8,128)(2,1)}, f32[512,512]{1,0:T(8,128)}, f32[128,5...) custom-call(bf16[128,1280]{1,0:T(8,128)(2,1)} %refs_0_.1, ...), custom_call_target="tpu_custom_call" | custom-call | tf_op jit(solution)/shard_map/pallas_call | solution.py:806
  80.9 3.5 %shard_map.223 = (bf16[512,1280]{1,0:T(8,128)(2,1)}, bf16[128,1280]{1,0:T(8,128)(2,1)}, bf16[512,1280]{1,0:T(8,128)(2,1)}, f32[512,512]{1,0:T(8,128)}, f32[128,5...) custom-call(bf16[512,1280]{1,0:T(8,128)(2,1)} %get-tuple-element.30., ...), custom_call_target="tpu_custom_call" | custom-call | tf_op jit(solution)/shard_map/pallas_call | solution.py:814
